TPU v7x, 128 devices: a whole 4x4x4 slice. The times are simulated.
128 devices in a mesh: chan: 16 (over z, x_hi, core), width: 8 (over y, x_lo).
Axes of the slice: x: 4 (x_hi: 2, x_lo: 2; x = x_hi * 2 + x_lo), y: 4, z: 4, core: 2. Of those that a mesh axis runs over, the one named last changes fastest.
Arguments:
- populations: float32 [19, 256, 128, 128], P(None, 'chan', 'width'), as said below
- moment_rates: float32 [15], replicated, may hold values from 0.8 to 1.9
- solid_flags: int32 [256, 128, 128], P('chan', 'width'), may hold values 0 or 1
- destination: int32 [524288, 1], P(('chan', 'width')), may hold values from 0 to 127; in each aligned block of 4096 rows (0 to 4095, 4096 to 8191, ...) at most 64 rows name the same one
- local_cell: int32 [524288], P(('chan', 'width')), may hold values from 0 to 32767
- particle_velocity: float32 [3, 524288], P(None, ('chan', 'width')), may hold values from -4 to 4
- coupling: float32 [524288], P(('chan', 'width')), may hold values from 0.05 to 0.5
Outputs:
- new_populations: float32 [19, 256, 128, 128], P(None, 'chan', 'width')
- new_particle_vel: float32 [3, 524288], P(None, ('chan', 'width'))
Inputs may be any that keep to these rules, and one draw needn't show every extreme that they name: `destination`: the particles held by one device name each device at most 64 times, and in every draw some device names some device exactly 64 times. `populations`: each entry is its direction's lattice weight times a factor between 0.1 and 1.9.
All inputs are finite; a program needn't handle non-finite values. No bound on the sum of `solid_flags` on one device may be relied on, other than what follows from the above.
Results may differ from a plain program's by a relative error of at most 0.0001.
Values sent between devices are 32-bit elements; how exact they have to be, the bound alone decides.
A program may use at most 128 MiB of HBM per device.

v0:
```python
import functools
import math

import jax
import jax.numpy as jnp
import numpy as np
from jax import lax
from jax.experimental import pallas as pl
from jax.experimental.pallas import tpu as pltpu
from jax.sharding import PartitionSpec as P

MESH = pl.DeviceIdType.MESH
STEPS = 4
CAP = 64
LATTICE = [
    [0, 0, 0],
    [1, 0, 0],
    [-1, 0, 0],
    [0, 1, 0],
    [0, -1, 0],
    [0, 0, 1],
    [0, 0, -1],
    [1, 1, 0],
    [-1, -1, 0],
    [1, -1, 0],
    [-1, 1, 0],
    [1, 0, 1],
    [-1, 0, -1],
    [1, 0, -1],
    [-1, 0, 1],
    [0, 1, 1],
    [0, -1, -1],
    [0, 1, -1],
    [0, -1, 1],
]
OPPOSITE = [0, 2, 1, 4, 3, 6, 5, 8, 7, 10, 9, 12, 11, 14, 13, 16, 15, 18, 17]
COUPLING_MASS = 0.02
RING = [9, 1, 11, 13, 7, 3, 15, 17, 10, 2, 12, 14, 8, 4, 16, 18]
SLOT_OF = {k: i for i, k in enumerate(RING)}
STAY = {0: 0, 5: 1, 6: 2}
PAD = 8
DIAGONALS = [(0, 1, 7), (0, 2, 11), (1, 2, 15)]


def moment_basis():
    lattice_np = np.array(LATTICE, dtype=np.float32)
    along_x, along_y, along_z = (lattice_np[:, 0], lattice_np[:, 1], lattice_np[:, 2])
    columns = [
        np.ones(19, dtype=np.float32),
        along_x,
        along_y,
        along_z,
        along_x * along_x,
        along_y * along_y,
        along_z * along_z,
        along_x * along_y,
        along_x * along_z,
        along_y * along_z,
        along_x * along_y * along_y,
        along_x * along_z * along_z,
        along_y * along_x * along_x,
        along_y * along_z * along_z,
        along_z * along_x * along_x,
        along_z * along_y * along_y,
        along_x * along_x * along_y * along_y,
        along_x * along_x * along_z * along_z,
        along_y * along_y * along_z * along_z,
    ]
    found_cols = []
    for column in columns:
        vector = np.array(column, dtype=np.float32)
        for repeat_pass in range(2):
            for earlier in found_cols:
                vector = vector - float(np.dot(earlier, vector)) * earlier
        found_cols.append((vector / math.sqrt(float(np.dot(vector, vector)))).astype(np.float32))
    return np.stack(found_cols[4:], axis=1).astype(np.float32)


def sector_tables():
    basis = moment_basis().astype(np.float64)

    def vec(entries):
        v = np.zeros(19)
        for k, s in entries:
            v[k] = s
        return v

    def project(members):
        m = np.stack(members)
        dots = m @ basis
        dots[np.abs(dots) < 1e-5] = 0.0
        sizes = np.sum(np.abs(m), axis=1)
        return dots[:, None, :] * dots[None, :, :] / sizes[None, :, None]

    even = [vec([(0, 1)])]
    for a in range(3):
        even.append(vec([(1 + 2 * a, 1), (2 + 2 * a, 1)]))
    for a, b, k in DIAGONALS:
        even.append(vec([(k + i, 1) for i in range(4)]))
    table = project(even)
    table = table[1:, 1:] - table[1:, :1]
    table[:3] *= 0.5
    table[3:] *= 0.25
    even_table = table
    odd_tables = []
    for a in range(3):
        members = [vec([(1 + 2 * a, 1), (2 + 2 * a, -1)])]
        for p, q, k in DIAGONALS:
            if a in (p, q):
                members.append(vec([(k + i, LATTICE[k + i][a]) for i in range(4)]))
        table = project(members)
        odd_tables.append((table[1:, 1:] - table[1:, :1]) * 0.25)
    cross = []
    for p, q, k in DIAGONALS:
        table = project([vec([(k + i, LATTICE[k + i][p] * LATTICE[k + i][q]) for i in range(4)])])
        cross.append(table[0, 0] * 0.25)
    return even_table, odd_tables, cross


def weigh(rates, weights):
    total = None
    for j in range(15):
        if abs(weights[j]) > 1e-9:
            term = rates[j] * float(weights[j])
            total = term if total is None else total + term
    return total if total is not None else rates[0] * 0.0


def split_bf16(x):
    hi = x.astype(jnp.bfloat16)
    lo = (x - hi.astype(jnp.float32)).astype(jnp.bfloat16)
    return hi, lo


def dot_nt(a, b):
    return lax.dot_general(a, b, (((1,), (1,)), ((), ())), preferred_element_type=jnp.float32)


def dot_nn(a, b):
    return lax.dot_general(a, b, (((1,), (0,)), ((), ())), preferred_element_type=jnp.float32)


def relax_group(f, fields, seen_m, solid, coef):
    even_c, odd_c, cross_c = coef
    sums, diffs = [], []
    for a in range(3):
        p, n = f[1 + 2 * a], f[2 + 2 * a]
        sums.append(p + n)
        diffs.append(p - n)
    diag_sum, diag_cross, diag_first, diag_second = [], [], [], []
    for p, q, k in DIAGONALS:
        a1, b1 = f[k] + f[k + 1], f[k] - f[k + 1]
        a2, b2 = f[k + 2] + f[k + 3], f[k + 2] - f[k + 3]
        diag_sum.append(a1 + a2)
        diag_cross.append(a1 - a2)
        diag_first.append(b1 + b2)
        diag_second.append(b1 - b2)
    odd = [[], [], []]
    for g, (p, q, k) in enumerate(DIAGONALS):
        odd[p].append(diag_first[g])
        odd[q].append(diag_second[g])
    mom = [diffs[a] + (odd[a][0] + odd[a][1]) for a in range(3)]
    density = f[0] + ((sums[0] + sums[1]) + sums[2]) + ((diag_sum[0] + diag_sum[1]) + diag_sum[2])
    count, held, memory = fields
    force = []
    for a in range(3):
        kept = held[a]
        for weight, earlier in zip(memory, seen_m):
            kept = kept + weight * earlier[a]
        force.append(COUPLING_MASS * (kept - count * mom[a]))
    half = [0.5 * force[a] for a in range(3)]
    vel = [mom[a] + half[a] for a in range(3)]
    press = [mom[a] * mom[a] - half[a] * half[a] for a in range(3)]
    press_sum = press[0] + press[1] + press[2]
    work = [vel[a] * force[a] for a in range(3)]
    work_third = (work[0] + work[1] + work[2]) * (1.0 / 3.0)
    base = density * (1.0 / 9.0) - press_sum * (1.0 / 6.0)
    gaps = []
    for a in range(3):
        gaps.append(base + 0.5 * press[a] - sums[a])
    for g, (p, q, k) in enumerate(DIAGONALS):
        gaps.append(base + 0.5 * (press[p] + press[q]) - diag_sum[g])
    change = []
    for a in range(6):
        total = even_c[a][0] * gaps[0]
        for b in range(1, 6):
            total = total + even_c[a][b] * gaps[b]
        if a < 3:
            total = total + 0.5 * (work[a] - work_third)
        else:
            p, q, k = DIAGONALS[a - 3]
            total = total + 0.25 * (work[p] + work[q] - work_third)
        change.append(total)
    rest = f[0] - 2.0 * (change[0] + change[1] + change[2]) - 4.0 * (change[3] + change[4] + change[5])
    odd_axis, odd_diag = [], []
    for a in range(3):
        third = mom[a] * (1.0 / 3.0)
        g1, g2 = third - odd[a][0], third - odd[a][1]
        d1 = odd_c[a][0][0] * g1 + odd_c[a][0][1] * g2
        d2 = odd_c[a][1][0] * g1 + odd_c[a][1][1] * g2
        push = force[a] * (1.0 / 12.0)
        odd_axis.append(2.0 * (push - (d1 + d2)))
        odd_diag.append([push + d1, push + d2])
    out = [None] * 19
    out[0] = rest
    for a in range(3):
        out[1 + 2 * a] = f[1 + 2 * a] + (change[a] + odd_axis[a])
        out[2 + 2 * a] = f[2 + 2 * a] + (change[a] - odd_axis[a])
    place = [0, 0, 0]
    for g, (p, q, k) in enumerate(DIAGONALS):
        o1, o2 = odd_diag[p][place[p]], odd_diag[q][place[q]]
        place[p] += 1
        place[q] += 1
        gap = mom[p] * mom[q] - half[p] * half[q] - diag_cross[g]
        cross = cross_c[g] * gap + 0.25 * (vel[p] * force[q] + vel[q] * force[p])
        s_plus, s_minus = change[3 + g] + cross, change[3 + g] - cross
        o_plus, o_minus = o1 + o2, o1 - o2
        out[k] = f[k] + (s_plus + o_plus)
        out[k + 1] = f[k + 1] + (s_plus - o_plus)
        out[k + 2] = f[k + 2] + (s_minus + o_minus)
        out[k + 3] = f[k + 3] + (s_minus - o_minus)
    out = [jnp.where(solid, f[OPPOSITE[k]], out[k]) for k in range(19)]
    return out, mom


def kernel(
    dims,
    pop_hbm,
    rates,
    solid_ref,
    dest_ref,
    cell_ref,
    vel_ref,
    coup_ref,
    out_hbm,
    vel_out,
    pop,
    outv,
    moved,
    stayed,
    own_hits,
    rank_rows,
    packing,
    send1,
    recv1,
    send2,
    recv2,
    slots,
    plane_hits,
    depth_hits,
    spread,
    summed,
    fields,
    mom,
    mom_t,
    coef_ref,
    pop_sem,
    out_sem,
    a2a_send,
    a2a_recv,
    halo_send,
    halo_recv,
):
    n_chan, n_width, size_x, size_y, size_z, parts = dims
    n_dev = n_chan * n_width
    rows = n_dev * CAP // 128
    planes = size_x * size_y
    chan, width = lax.axis_index("chan"), lax.axis_index("width")
    me = chan * n_width + width
    f32, bf16, i32 = jnp.float32, jnp.bfloat16, jnp.int32

    barrier = pltpu.get_barrier_semaphore()

    def greet(i, _):
        o = lax.rem(me + i, n_dev)
        pl.semaphore_signal(
            barrier, inc=1, device_id=(o // n_width, lax.rem(o, n_width)), device_id_type=MESH
        )
        return 0

    lax.fori_loop(1, n_dev, greet, 0)
    pop_copy = pltpu.make_async_copy(pop_hbm, pop, pop_sem)
    pop_copy.start()

    even_table, odd_tables, cross_table = sector_tables()
    places = 0
    for a in range(6):
        for b in range(6):
            coef_ref[places] = weigh(rates, even_table[a, b])
            places += 1
    for axis in range(3):
        for a in range(2):
            for b in range(2):
                coef_ref[places] = weigh(rates, odd_tables[axis][a, b])
                places += 1
    for g in range(3):
        coef_ref[places] = weigh(rates, cross_table[g])
        places += 1

    block = 256
    tri = (
        lax.broadcasted_iota(i32, (block, block), 0) <= lax.broadcasted_iota(i32, (block, block), 1)
    ).astype(f32).astype(bf16)
    dev_iota = lax.broadcasted_iota(i32, (n_dev, block), 0)
    cap_iota = lax.broadcasted_iota(i32, (CAP, block), 0).astype(f32)

    def pack(b, before):
        s = pl.ds(pl.multiple_of(b * block, block), block)
        hits = jnp.where(dev_iota == dest_ref[:, s], 1.0, 0.0)
        hits_b = hits.astype(bf16)
        own_hits[:, s] = hits_b
        upto = dot_nn(hits_b, tri)
        rank = jnp.sum(hits * (upto + before), axis=0, keepdims=True) - 1.0
        rank_rows[:, s] = rank
        rank_hit = cap_iota == rank
        cell = cell_ref[:, s]
        pieces = []
        for value in (coup_ref[:, s], vel_ref[0:1, s], vel_ref[1:2, s], vel_ref[2:3, s]):
            pieces.append(split_bf16(value))
        order = [pieces[0][0], pieces[1][0], pieces[0][1], pieces[1][1]]
        order += [pieces[2][0], pieces[3][0], pieces[2][1], pieces[3][1]]
        order = [piece.astype(f32) for piece in order]
        order += [(cell // 128).astype(f32), lax.rem(cell, 128).astype(f32)]
        for j, row in enumerate(order):
            packing[j * CAP : (j + 1) * CAP, s] = jnp.where(rank_hit, row, 0.0).astype(bf16)
        return before + upto[:, block - 1 : block]

    lax.fori_loop(0, parts // block, pack, jnp.zeros((n_dev, 1), f32))
    packed = dot_nt(own_hits[...], packing[...])
    low = lax.broadcasted_iota(i32, (n_dev, 128), 1) < 64
    send1[0] = packed[:, 0:128] + packed[:, 128:256]
    send1[1] = packed[:, 256:384] + packed[:, 384:512]
    last = packed[:, 512:640]
    send1[2] = jnp.where(low, last * 128.0 + pltpu.roll(last, 64, 1), 0.0)

    pl.semaphore_wait(barrier, n_dev - 1)

    def exchange_start(src, dst, which):
        def send(i, _):
            o = lax.rem(me + i, n_dev)
            pltpu.make_async_remote_copy(
                src.at[:, pl.ds(o, 1)],
                dst.at[:, pl.ds(me, 1)],
                a2a_send.at[which],
                a2a_recv.at[which],
                device_id=(o // n_width, lax.rem(o, n_width)),
                device_id_type=MESH,
            ).start()
            return 0

        lax.fori_loop(1, n_dev, send, 0)
        dst[:, pl.ds(me, 1), :] = src[:, pl.ds(me, 1), :]

    def exchange_wait(src, dst, which):
        part = pl.ds(0, n_dev - 1)
        pltpu.make_async_copy(dst.at[:, part], dst.at[:, part], a2a_recv.at[which]).wait()
        pltpu.make_async_copy(src.at[:, part], src.at[:, part], a2a_send.at[which]).wait()

    exchange_start(send1, recv1, 0)
    exchange_wait(send1, recv1, 0)

    half_dev = n_dev // 2
    low = lax.broadcasted_iota(i32, (half_dev, 128), 1) < 64

    def both(ref):
        first, second = ref[0:half_dev, :], ref[half_dev:n_dev, :]
        return (
            jnp.where(low, first, pltpu.roll(second, 64, 1)),
            jnp.where(low, pltpu.roll(first, 64, 1), second),
        )

    coup, vx = both(recv1[0])
    vy, vz = both(recv1[1])
    cell = both(recv1[2])[0].astype(i32)
    slots[0], slots[1], slots[2], slots[3] = coup, vx, vy, vz
    slots[4] = (cell // 128).astype(f32)
    slots[5] = lax.rem(cell, 128).astype(f32)
    slots[6], slots[7], slots[8] = coup * vx, coup * vy, coup * vz
    slots[9] = coup

    plane_iota = lax.broadcasted_iota(i32, (planes, 128), 0).astype(f32)
    depth_iota = lax.broadcasted_iota(i32, (size_z, 128), 0).astype(f32)

    def place(i, _):
        s = pl.ds(pl.multiple_of(i * 128, 128), 128)
        plane_hits[:, s] = jnp.where(plane_iota == slots[4, pl.ds(i, 1), :], 1.0, 0.0).astype(bf16)
        depth_hits[:, s] = jnp.where(depth_iota == slots[5, pl.ds(i, 1), :], 1.0, 0.0).astype(bf16)
        return 0

    lax.fori_loop(0, rows, place, 0)

    chunk = min(1024, rows * 128)
    chunk_rows = chunk // 128

    def scatter(targets):
        summed[...] = jnp.zeros_like(summed)

        def one(n, _):
            for r in range(chunk_rows):
                i = n * chunk_rows + r
                hits = depth_hits[:, pl.ds(pl.multiple_of(i * 128, 128), 128)]
                hits = hits.reshape(size_z // 16, 16, 128)
                for j in range(4):
                    value = jnp.broadcast_to(slots[6 + j, pl.ds(i, 1), :], (16, 128))
                    for h, piece in enumerate(split_bf16(value)):
                        at = (2 * j + h) * size_z
                        spread[at : at + size_z, r * 128 : (r + 1) * 128] = (
                            hits * piece[None]
                        ).reshape(size_z, 128)
            s = pl.ds(pl.multiple_of(n * chunk, chunk), chunk)
            summed[...] += dot_nt(plane_hits[:, s], spread[...])
            return 0

        lax.fori_loop(0, rows // chunk_rows, one, 0)
        for j, target in enumerate(targets):
            at = 2 * j * size_z
            fields[target] = summed[:, at : at + size_z] + summed[:, at + size_z : at + 2 * size_z]

    def gather(t):
        for a in range(3):
            hi, lo = split_bf16(mom[t, a].T)
            mom_t[a * size_z : (a + 1) * size_z, :] = hi
            mom_t[(3 + a) * size_z : (4 + a) * size_z, :] = lo

        def one(n, _):
            s = pl.ds(pl.multiple_of(n * 256, 256), 256)
            found = dot_nn(mom_t[...], plane_hits[:, s])
            for r in range(2):
                i = 2 * n + r
                hit = depth_iota == slots[5, pl.ds(i, 1), :]
                c = slots[0, pl.ds(i, 1), :]
                lanes = slice(r * 128, (r + 1) * 128)
                for a in range(3):
                    both = (
                        found[a * size_z : (a + 1) * size_z, lanes]
                        + found[(3 + a) * size_z : (4 + a) * size_z, lanes]
                    )
                    seen = jnp.sum(jnp.where(hit, both, 0.0), axis=0, keepdims=True)
                    v = slots[1 + a, pl.ds(i, 1), :]
                    slots[1 + a, pl.ds(i, 1), :] = v + c * (seen - v)
            return 0

        lax.fori_loop(0, rows // 2, one, 0)

    def nb(dc, dw):
        return (lax.rem(chan + dc + n_chan, n_chan), lax.rem(width + dw + n_width, n_width))

    inner_x, inner_y = pl.ds(1, size_x), pl.ds(PAD, size_y)
    last_x, last_y = size_x, PAD + size_y - 1
    end_x, end_y = size_x + 1, PAD + size_y

    def halo_copies(t):
        g = moved.at[t % 2]
        parts_list = [
            (g.at[0:5, last_x, inner_y], g.at[0:5, 0, inner_y], nb(1, 0)),
            (g.at[8:13, 1, inner_y], g.at[8:13, end_x, inner_y], nb(-1, 0)),
            (g.at[4:9, inner_x, last_y], g.at[4:9, inner_x, PAD - 1], nb(0, 1)),
            (g.at[12:16, inner_x, PAD], g.at[12:16, inner_x, end_y], nb(0, -1)),
            (g.at[0:1, inner_x, PAD], g.at[0:1, inner_x, end_y], nb(0, -1)),
            (g.at[4, last_x, pl.ds(last_y, 1)], g.at[4, 0, pl.ds(PAD - 1, 1)], nb(1, 1)),
            (g.at[12, 1, pl.ds(PAD, 1)], g.at[12, end_x, pl.ds(end_y, 1)], nb(-1, -1)),
            (g.at[0, last_x, pl.ds(PAD, 1)], g.at[0, 0, pl.ds(end_y, 1)], nb(1, -1)),
            (g.at[8, 1, pl.ds(last_y, 1)], g.at[8, end_x, pl.ds(PAD - 1, 1)], nb(-1, 1)),
        ]
        return [
            pltpu.make_async_remote_copy(
                src, dst, halo_send.at[t, n], halo_recv.at[t, n], device_id=to, device_id_type=MESH
            )
            for n, (src, dst, to) in enumerate(parts_list)
        ]

    def load(t, i, h):
        f = []
        for k in range(19):
            if t == 0:
                f.append(pop[k, i, 8 * h : 8 * h + 8, :])
            elif k in STAY:
                f.append(stayed[(t - 1) % 2, STAY[k], i, 8 * h : 8 * h + 8, :])
            else:
                step_x, step_y, _ = LATTICE[k]
                start = PAD + 8 * h - step_y
                f.append(moved[(t - 1) % 2, SLOT_OF[k], i + 1 - step_x, start : start + 8, :])
        return f

    def step(t):
        def one(i, _):
            coef = [coef_ref[n] for n in range(51)]
            even_c = [coef[6 * a : 6 * a + 6] for a in range(6)]
            odd_c = [
                [coef[36 + 4 * a : 38 + 4 * a], coef[38 + 4 * a : 40 + 4 * a]] for a in range(3)
            ]
            coefs = (even_c, odd_c, coef[48:51])
            for h in range(size_y // 8):
                f = load(t, i, h)
                at = pl.ds(pl.multiple_of(i * size_y + 8 * h, 8), 8)
                count = fields[0, at, :]
                held = [fields[1 + a, at, :] for a in range(3)]
                memory = [fields[4 + t - 1 - s, at, :] for s in range(t)]
                seen_m = [[mom[s, a, at, :] for a in range(3)] for s in range(t)]
                solid = solid_ref[i, 8 * h : 8 * h + 8, :] == 1
                out, m = relax_group(f, (count, held, memory), seen_m, solid, coefs)
                for a in range(3):
                    mom[t, a, at, :] = m[a]
                for k in range(19):
                    value = out[k]
                    if LATTICE[k][2]:
                        value = pltpu.roll(value, LATTICE[k][2] % size_z, 1)
                    if k in STAY:
                        stayed[t % 2, STAY[k], i, 8 * h : 8 * h + 8, :] = value
                    else:
                        moved[t % 2, SLOT_OF[k], i + 1, PAD + 8 * h : PAD + 8 * h + 8, :] = value
            return 0

        lax.fori_loop(0, size_x, one, 0)

    scatter([1, 2, 3, 0])
    coup = slots[0]
    keep = 1.0 - coup
    slots[9] = coup * coup
    pop_copy.wait()
    for t in range(STEPS):
        step(t)
        copies = halo_copies(t)
        for copy in copies:
            copy.start()
        gather(t)
        if t < STEPS - 1:
            for a in range(3):
                slots[6 + a] = slots[6 + a] * keep
            if t > 0:
                slots[9] = slots[9] * keep
            scatter([1, 2, 3, 4 + t])
        else:
            low = lax.broadcasted_iota(i32, (half_dev, 128), 1) < 64
            vx, vy, vz = slots[1], slots[2], slots[3]
            send2[0, 0:half_dev, :] = jnp.where(low, vx, pltpu.roll(vy, 64, 1))
            send2[0, half_dev:n_dev, :] = jnp.where(low, pltpu.roll(vx, 64, 1), vy)
            send2[1, 0:half_dev, :] = jnp.where(low, vz, 0.0)
            send2[1, half_dev:n_dev, :] = jnp.where(low, pltpu.roll(vz, 64, 1), 0.0)
            exchange_start(send2, recv2, 1)
        for copy in copies:
            copy.wait()

    def finish(i, _):
        for h in range(size_y // 8):
            f = load(STEPS, i, h)
            for k in range(19):
                outv[k, i, 8 * h : 8 * h + 8, :] = f[k]
        return 0

    lax.fori_loop(0, size_x, finish, 0)
    out_copy = pltpu.make_async_copy(outv, out_hbm, out_sem)
    out_copy.start()
    exchange_wait(send2, recv2, 1)

    back = [split_bf16(recv2[a].T) for a in range(2)]
    back = jnp.concatenate(
        [back[0][0], back[1][0][0:64], back[0][1], back[1][1][0:64]], axis=0
    )

    def unpack(b, _):
        s = pl.ds(pl.multiple_of(b * block, block), block)
        found = dot_nn(back, own_hits[:, s])
        hit = cap_iota == rank_rows[:, s]
        for a in range(3):
            value = found[64 * a : 64 * a + 64] + found[64 * (a + 3) : 64 * (a + 3) + 64]
            vel_out[a : a + 1, s] = jnp.sum(jnp.where(hit, value, 0.0), axis=0, keepdims=True)
        return 0

    lax.fori_loop(0, parts // block, unpack, 0)
    out_copy.wait()


def per_device(
    n_chan,
    n_width,
    populations,
    moment_rates,
    solid_flags,
    destination,
    local_cell,
    particle_velocity,
    coupling,
):
    _, size_x, size_y, size_z = populations.shape
    parts = destination.shape[0]
    n_dev = n_chan * n_width
    rows = n_dev * CAP // 128
    planes = size_x * size_y
    f32, bf16 = jnp.float32, jnp.bfloat16
    vmem = pl.BlockSpec(memory_space=pltpu.VMEM)
    chunk = min(1024, rows * 128)
    return pl.pallas_call(
        functools.partial(kernel, (n_chan, n_width, size_x, size_y, size_z, parts)),
        out_shape=(
            jax.ShapeDtypeStruct(populations.shape, f32),
            jax.ShapeDtypeStruct(particle_velocity.shape, f32),
        ),
        in_specs=[
            pl.BlockSpec(memory_space=pl.ANY),
            pl.BlockSpec(memory_space=pltpu.SMEM),
            vmem,
            vmem,
            vmem,
            vmem,
            vmem,
        ],
        out_specs=(pl.BlockSpec(memory_space=pl.ANY), vmem),
        scratch_shapes=[
            pltpu.VMEM(populations.shape, f32),
            pltpu.VMEM(populations.shape, f32),
            pltpu.VMEM((2, 16, size_x + 2, size_y + 2 * PAD, size_z), f32),
            pltpu.VMEM((2, 3, size_x, size_y, size_z), f32),
            pltpu.VMEM((n_dev, parts), bf16),
            pltpu.VMEM((1, parts), f32),
            pltpu.VMEM((10 * CAP, parts), bf16),
            pltpu.VMEM((3, n_dev, 128), f32),
            pltpu.VMEM((3, n_dev, 128), f32),
            pltpu.VMEM((2, n_dev, 128), f32),
            pltpu.VMEM((2, n_dev, 128), f32),
            pltpu.VMEM((10, rows, 128), f32),
            pltpu.VMEM((planes, rows * 128), bf16),
            pltpu.VMEM((size_z, rows * 128), bf16),
            pltpu.VMEM((8 * size_z, chunk), bf16),
            pltpu.VMEM((planes, 8 * size_z), f32),
            pltpu.VMEM((7, planes, size_z), f32),
            pltpu.VMEM((STEPS, 3, planes, size_z), f32),
            pltpu.VMEM((6 * size_z, planes), bf16),
            pltpu.SMEM((64,), f32),
            pltpu.SemaphoreType.DMA,
            pltpu.SemaphoreType.DMA,
            pltpu.SemaphoreType.DMA((2,)),
            pltpu.SemaphoreType.DMA((2,)),
            pltpu.SemaphoreType.DMA((STEPS, 9)),
            pltpu.SemaphoreType.DMA((STEPS, 9)),
        ],
        compiler_params=pltpu.CompilerParams(
            collective_id=0, has_side_effects=True, vmem_limit_bytes=56 * 1024 * 1024
        ),
        name="lattice_steps",
    )(
        populations,
        moment_rates,
        solid_flags,
        destination.reshape(1, parts),
        local_cell.reshape(1, parts),
        particle_velocity,
        coupling.reshape(1, parts),
    )


def solution(mesh):
    return jax.shard_map(
        functools.partial(per_device, mesh.shape["chan"], mesh.shape["width"]),
        mesh=mesh,
        in_specs=(
            P(None, "chan", "width", None),
            P(),
            P("chan", "width", None),
            P(("chan", "width"), None),
            P(("chan", "width")),
            P(None, ("chan", "width")),
            P(("chan", "width")),
        ),
        out_specs=(P(None, "chan", "width", None), P(None, ("chan", "width"))),
        check_vma=False,
    )
```

profile of v0, /device:TPU:1, one launch (start us, length us, event | category | flops | bytes accessed | tf_op | source)
XLA Modules:
  0.0 114.9 jit_solution(14915471505350265006)
XLA Ops:
  0.6 110.2 %lattice_steps.1 = (f32[19,16,16,128]{3,2,1,0:T(8,128)}, f32[3,4096]{1,0:T(4,128)}) custom-call(f32[19,16,16,128]{3,2,1,0:T(8,128)} %pop_hbm.1, f32[15]{0:T(128)} %rates.1, s32[16,16,128]{2,1,0:T(8,128)} %solid_ref.1, s32[1,4096]{1,0:T(1,128)} %bitcast.3, s32[1,4096]{1,0:T(1,128)} %bitcast.4, f32[3,4096]{1,0:T(4,128)} %vel_ref.1, f32[1,4096]{1,0:T(1,128)} %bitcast.5), custom_call_target="tpu_custom_call" | custom-call | tf_op jit(solution)/shard_map/lattice_steps/pallas_call | solution.py:593
  110.9 0.0 copy-start
  110.9 3.4 %copy.11 = f32[19,16,16,128]{3,2,1,0:T(8,128)} copy(f32[19,16,16,128]{3,2,1,0:T(8,128)} %get-tuple-element.4) | data formatting | bytes 4980736
  114.3 0.0 copy-done
  114.3 0.6 copy.12
Async XLA Ops:
  110.9 3.4 %copy-start = (f32[3,4096]{1,0:T(4,128)S(1)}, f32[3,4096]{1,0:T(4,128)}, u32[]{:S(2)}) copy-start(f32[3,4096]{1,0:T(4,128)} %get-tuple-element.5) | copy-start | bytes 147460
where the time goes:
time: 115 us
  Pallas kernels  110 us (96%)
  local copies, waits for them, and re-layouts  4.03 us (4%)
    pallas_call x1, Pallas kernels, per_device(): pl.pallas_call(functools.partial(kernel, (n_chan, n_width, size_x, size_y...  110 us
    unnamed x4, local copies, waits for them, and re-layouts  4.03 us

commit v1 on v0

--- a/solution.py
+++ b/solution.py
@@ -123,7 +123,7 @@
         if abs(weights[j]) > 1e-9:
             term = rates[j] * float(weights[j])
             total = term if total is None else total + term
-    return total if total is not None else rates[0] * 0.0
+    return total if total is not None else jnp.zeros_like(rates[0])
 
 
 def split_bf16(x):
@@ -226,30 +226,35 @@
 def kernel(
     dims,
     pop_hbm,
-    rates,
+    rates_ref,
     solid_ref,
     dest_ref,
     cell_ref,
     vel_ref,
     coup_ref,
     out_hbm,
-    vel_out,
+    back_out,
+    rank_rows,
     pop,
-    outv,
     moved,
     stayed,
     own_hits,
-    rank_rows,
     packing,
     send1,
     recv1,
     send2,
     recv2,
     slots,
+    cells,
+    weights,
+    seen,
     plane_hits,
     depth_hits,
-    spread,
+    spread_a,
+    spread_b,
     summed,
+    found_a,
+    found_b,
     fields,
     mom,
     mom_t,
@@ -283,6 +288,7 @@
     pop_copy.start()
 
     even_table, odd_tables, cross_table = sector_tables()
+    rates = [jnp.full((8, 128), rates_ref[j], f32) for j in range(15)]
     places = 0
     for a in range(6):
         for b in range(6):
@@ -325,7 +331,7 @@
             packing[j * CAP : (j + 1) * CAP, s] = jnp.where(rank_hit, row, 0.0).astype(bf16)
         return before + upto[:, block - 1 : block]
 
-    lax.fori_loop(0, parts // block, pack, jnp.zeros((n_dev, 1), f32))
+    lax.fori_loop(0, parts // block, pack, jnp.zeros((n_dev, 1), f32), unroll=4)
     packed = dot_nt(own_hits[...], packing[...])
     low = lax.broadcasted_iota(i32, (n_dev, 128), 1) < 64
     send1[0] = packed[:, 0:128] + packed[:, 128:256]
@@ -335,28 +341,27 @@
 
     pl.semaphore_wait(barrier, n_dev - 1)
 
-    def exchange_start(src, dst, which):
-        def send(i, _):
-            o = lax.rem(me + i, n_dev)
-            pltpu.make_async_remote_copy(
-                src.at[:, pl.ds(o, 1)],
-                dst.at[:, pl.ds(me, 1)],
-                a2a_send.at[which],
-                a2a_recv.at[which],
-                device_id=(o // n_width, lax.rem(o, n_width)),
-                device_id_type=MESH,
-            ).start()
-            return 0
-
-        lax.fori_loop(1, n_dev, send, 0)
-        dst[:, pl.ds(me, 1), :] = src[:, pl.ds(me, 1), :]
+    def exchange_send(src, dst, which, o):
+        pltpu.make_async_remote_copy(
+            src.at[:, pl.ds(o, 1)],
+            dst.at[:, pl.ds(me, 1)],
+            a2a_send.at[which],
+            a2a_recv.at[which],
+            device_id=(o // n_width, lax.rem(o, n_width)),
+            device_id_type=MESH,
+        ).start()
 
     def exchange_wait(src, dst, which):
         part = pl.ds(0, n_dev - 1)
         pltpu.make_async_copy(dst.at[:, part], dst.at[:, part], a2a_recv.at[which]).wait()
         pltpu.make_async_copy(src.at[:, part], src.at[:, part], a2a_send.at[which]).wait()
 
-    exchange_start(send1, recv1, 0)
+    def send_one(i, _):
+        exchange_send(send1, recv1, 0, lax.rem(me + i, n_dev))
+        return 0
+
+    lax.fori_loop(1, n_dev, send_one, 0)
+    recv1[:, pl.ds(me, 1), :] = send1[:, pl.ds(me, 1), :]
     exchange_wait(send1, recv1, 0)
 
     half_dev = n_dev // 2
@@ -373,74 +378,137 @@
     vy, vz = both(recv1[1])
     cell = both(recv1[2])[0].astype(i32)
     slots[0], slots[1], slots[2], slots[3] = coup, vx, vy, vz
-    slots[4] = (cell // 128).astype(f32)
-    slots[5] = lax.rem(cell, 128).astype(f32)
-    slots[6], slots[7], slots[8] = coup * vx, coup * vy, coup * vz
-    slots[9] = coup
+    cells[0] = (cell // 128).astype(f32)
+    cells[1] = lax.rem(cell, 128).astype(f32)
+    weights[0], weights[1], weights[2] = coup * vx, coup * vy, coup * vz
+    weights[3] = coup
 
     plane_iota = lax.broadcasted_iota(i32, (planes, 128), 0).astype(f32)
     depth_iota = lax.broadcasted_iota(i32, (size_z, 128), 0).astype(f32)
 
     def place(i, _):
         s = pl.ds(pl.multiple_of(i * 128, 128), 128)
-        plane_hits[:, s] = jnp.where(plane_iota == slots[4, pl.ds(i, 1), :], 1.0, 0.0).astype(bf16)
-        depth_hits[:, s] = jnp.where(depth_iota == slots[5, pl.ds(i, 1), :], 1.0, 0.0).astype(bf16)
+        hits = jnp.where(plane_iota == cells[0, pl.ds(i, 1), :], 1.0, 0.0).astype(bf16)
+        plane_hits[0:planes, s] = hits
+        plane_hits[planes : 2 * planes, s] = hits
+        depth_hits[:, s] = jnp.where(depth_iota == cells[1, pl.ds(i, 1), :], 1.0, 0.0).astype(bf16)
         return 0
 
-    lax.fori_loop(0, rows, place, 0)
-
-    chunk = min(1024, rows * 128)
+    lax.fori_loop(0, rows, place, 0, unroll=2)
+
+    chunk = min(2048, rows * 128 // 2)
     chunk_rows = chunk // 128
 
-    def scatter(targets):
+    chunks = rows // chunk_rows
+
+    def weigh_chunk(n, spread):
+        for r in range(chunk_rows):
+            i = n * chunk_rows + r
+            hits = depth_hits[:, pl.ds(pl.multiple_of(i * 128, 128), 128)]
+            hits = hits.reshape(size_z // 16, 16, 128)
+            for j in range(4):
+                value = jnp.broadcast_to(weights[j, pl.ds(i, 1), :], (16, 128))
+                for h, piece in enumerate(split_bf16(value)):
+                    at = (2 * j + h) * size_z
+                    spread[at : at + size_z, r * 128 : (r + 1) * 128] = (
+                        hits * piece[None]
+                    ).reshape(size_z, 128)
+
+    def add_chunk(n, spread):
+        s = pl.ds(pl.multiple_of(n * chunk, chunk), chunk)
+        summed[...] += dot_nt(spread[...], plane_hits[0:planes, s])
+
+    def scatter(targets, beside=None):
         summed[...] = jnp.zeros_like(summed)
-
-        def one(n, _):
-            for r in range(chunk_rows):
-                i = n * chunk_rows + r
-                hits = depth_hits[:, pl.ds(pl.multiple_of(i * 128, 128), 128)]
-                hits = hits.reshape(size_z // 16, 16, 128)
-                for j in range(4):
-                    value = jnp.broadcast_to(slots[6 + j, pl.ds(i, 1), :], (16, 128))
-                    for h, piece in enumerate(split_bf16(value)):
-                        at = (2 * j + h) * size_z
-                        spread[at : at + size_z, r * 128 : (r + 1) * 128] = (
-                            hits * piece[None]
-                        ).reshape(size_z, 128)
-            s = pl.ds(pl.multiple_of(n * chunk, chunk), chunk)
-            summed[...] += dot_nt(plane_hits[:, s], spread[...])
+        weigh_chunk(0, spread_a)
+        share = size_x // chunks
+
+        def two(n, _):
+            weigh_chunk(2 * n + 1, spread_b)
+            add_chunk(2 * n, spread_a)
+            if beside is not None:
+                for i in range(share):
+                    beside(2 * n * share + i)
+            weigh_chunk(lax.rem(2 * n + 2, chunks), spread_a)
+            add_chunk(2 * n + 1, spread_b)
+            if beside is not None:
+                for i in range(share):
+                    beside((2 * n + 1) * share + i)
             return 0
 
-        lax.fori_loop(0, rows // chunk_rows, one, 0)
+        lax.fori_loop(0, chunks // 2, two, 0)
         for j, target in enumerate(targets):
             at = 2 * j * size_z
-            fields[target] = summed[:, at : at + size_z] + summed[:, at + size_z : at + 2 * size_z]
-
-    def gather(t):
+            total = summed[at : at + size_z, :] + summed[at + size_z : at + 2 * size_z, :]
+            fields[target] = total.T
+
+    tile = min(1024, rows * 128 // 2)
+    tile_rows = tile // 128
+
+    def find(n, found):
+        s = pl.ds(pl.multiple_of(n * tile, tile), tile)
+        found[...] = dot_nn(mom_t[...], plane_hits[:, s])
+
+    def pick(n, found):
+        for r in range(tile_rows):
+            i = n * tile_rows + r
+            hit = depth_iota == cells[1, pl.ds(i, 1), :]
+            for a in range(3):
+                both = found[a * size_z : (a + 1) * size_z, r * 128 : (r + 1) * 128]
+                seen[a, pl.ds(i, 1), :] = jnp.sum(
+                    jnp.where(hit, both, 0.0), axis=0, keepdims=True
+                )
+
+    tiles = rows // tile_rows
+    first_tile = lax.rem(me, rows) // tile_rows
+
+    def gather(t, then=None):
         for a in range(3):
             hi, lo = split_bf16(mom[t, a].T)
-            mom_t[a * size_z : (a + 1) * size_z, :] = hi
-            mom_t[(3 + a) * size_z : (4 + a) * size_z, :] = lo
-
-        def one(n, _):
-            s = pl.ds(pl.multiple_of(n * 256, 256), 256)
-            found = dot_nn(mom_t[...], plane_hits[:, s])
-            for r in range(2):
-                i = 2 * n + r
-                hit = depth_iota == slots[5, pl.ds(i, 1), :]
-                c = slots[0, pl.ds(i, 1), :]
-                lanes = slice(r * 128, (r + 1) * 128)
-                for a in range(3):
-                    both = (
-                        found[a * size_z : (a + 1) * size_z, lanes]
-                        + found[(3 + a) * size_z : (4 + a) * size_z, lanes]
-                    )
-                    seen = jnp.sum(jnp.where(hit, both, 0.0), axis=0, keepdims=True)
-                    v = slots[1 + a, pl.ds(i, 1), :]
-                    slots[1 + a, pl.ds(i, 1), :] = v + c * (seen - v)
+            mom_t[a * size_z : (a + 1) * size_z, 0:planes] = hi
+            mom_t[a * size_z : (a + 1) * size_z, planes : 2 * planes] = lo
+
+        def turn(n):
+            return n if then is None else lax.rem(n + first_tile, tiles)
+
+        find(turn(0), found_a)
+
+        def two(n, _):
+            first, second, third = turn(2 * n), turn(2 * n + 1), turn(lax.rem(2 * n + 2, tiles))
+            find(second, found_b)
+            pick(first, found_a)
+            if then is not None:
+                then(first)
+            find(third, found_a)
+            pick(second, found_b)
+            if then is not None:
+                then(second)
             return 0
 
-        lax.fori_loop(0, rows // 2, one, 0)
+        lax.fori_loop(0, tiles // 2, two, 0)
+        if then is None:
+            for a in range(3):
+                slots[1 + a] = slots[1 + a] + slots[0] * (seen[a] - slots[1 + a])
+
+    def deliver(n):
+        s = pl.ds(pl.multiple_of(n * tile_rows, tile_rows), tile_rows)
+        upper = pl.ds(pl.multiple_of(half_dev + n * tile_rows, tile_rows), tile_rows)
+        low = lax.broadcasted_iota(i32, (tile_rows, 128), 1) < 64
+        c = slots[0, s, :]
+        vx, vy, vz = [
+            slots[1 + a, s, :] + c * (seen[a, s, :] - slots[1 + a, s, :]) for a in range(3)
+        ]
+        send2[0, s, :] = jnp.where(low, vx, pltpu.roll(vy, 64, 1))
+        send2[0, upper, :] = jnp.where(low, pltpu.roll(vx, 64, 1), vy)
+        send2[1, s, :] = jnp.where(low, vz, 0.0)
+        send2[1, upper, :] = jnp.where(low, pltpu.roll(vz, 64, 1), 0.0)
+        for r in range(tile_rows):
+            for side in range(2):
+                o = side * half_dev + n * tile_rows + r
+
+                @pl.when(o != me)
+                def _():
+                    exchange_send(send2, recv2, 1, o)
 
     def nb(dc, dw):
         return (lax.rem(chan + dc + n_chan, n_chan), lax.rem(width + dw + n_width, n_width))
@@ -482,8 +550,8 @@
                 f.append(moved[(t - 1) % 2, SLOT_OF[k], i + 1 - step_x, start : start + 8, :])
         return f
 
-    def step(t):
-        def one(i, _):
+    def step_plane(t):
+        def one(i):
             coef = [coef_ref[n] for n in range(51)]
             even_c = [coef[6 * a : 6 * a + 6] for a in range(6)]
             odd_c = [
@@ -494,8 +562,8 @@
                 f = load(t, i, h)
                 at = pl.ds(pl.multiple_of(i * size_y + 8 * h, 8), 8)
                 count = fields[0, at, :]
-                held = [fields[1 + a, at, :] for a in range(3)]
-                memory = [fields[4 + t - 1 - s, at, :] for s in range(t)]
+                held = [fields[1 + 3 * (t % 2) + a, at, :] for a in range(3)]
+                memory = [fields[7 + t - 1 - s, at, :] for s in range(t)]
                 seen_m = [[mom[s, a, at, :] for a in range(3)] for s in range(t)]
                 solid = solid_ref[i, 8 * h : 8 * h + 8, :] == 1
                 out, m = relax_group(f, (count, held, memory), seen_m, solid, coefs)
@@ -509,35 +577,37 @@
                         stayed[t % 2, STAY[k], i, 8 * h : 8 * h + 8, :] = value
                     else:
                         moved[t % 2, SLOT_OF[k], i + 1, PAD + 8 * h : PAD + 8 * h + 8, :] = value
-            return 0
-
-        lax.fori_loop(0, size_x, one, 0)
+
+        return one
 
     scatter([1, 2, 3, 0])
     coup = slots[0]
     keep = 1.0 - coup
-    slots[9] = coup * coup
+    weights[3] = coup * coup
     pop_copy.wait()
     for t in range(STEPS):
-        step(t)
+        plane = step_plane(t)
+        if t < STEPS - 1:
+            for a in range(3):
+                weights[a] = weights[a] * keep
+            if t > 0:
+                weights[3] = weights[3] * keep
+            odd = (t + 1) % 2
+            scatter([1 + 3 * odd, 2 + 3 * odd, 3 + 3 * odd, 7 + t], plane)
+        else:
+
+            def one(i, _):
+                plane(i)
+                return 0
+
+            lax.fori_loop(0, size_x, one, 0)
         copies = halo_copies(t)
         for copy in copies:
             copy.start()
-        gather(t)
         if t < STEPS - 1:
-            for a in range(3):
-                slots[6 + a] = slots[6 + a] * keep
-            if t > 0:
-                slots[9] = slots[9] * keep
-            scatter([1, 2, 3, 4 + t])
+            gather(t)
         else:
-            low = lax.broadcasted_iota(i32, (half_dev, 128), 1) < 64
-            vx, vy, vz = slots[1], slots[2], slots[3]
-            send2[0, 0:half_dev, :] = jnp.where(low, vx, pltpu.roll(vy, 64, 1))
-            send2[0, half_dev:n_dev, :] = jnp.where(low, pltpu.roll(vx, 64, 1), vy)
-            send2[1, 0:half_dev, :] = jnp.where(low, vz, 0.0)
-            send2[1, half_dev:n_dev, :] = jnp.where(low, pltpu.roll(vz, 64, 1), 0.0)
-            exchange_start(send2, recv2, 1)
+            gather(t, deliver)
         for copy in copies:
             copy.wait()
 
@@ -545,30 +615,52 @@
         for h in range(size_y // 8):
             f = load(STEPS, i, h)
             for k in range(19):
-                outv[k, i, 8 * h : 8 * h + 8, :] = f[k]
+                pop[k, i, 8 * h : 8 * h + 8, :] = f[k]
         return 0
 
     lax.fori_loop(0, size_x, finish, 0)
-    out_copy = pltpu.make_async_copy(outv, out_hbm, out_sem)
+    out_copy = pltpu.make_async_copy(pop, out_hbm, out_sem)
     out_copy.start()
+    recv2[:, pl.ds(me, 1), :] = send2[:, pl.ds(me, 1), :]
     exchange_wait(send2, recv2, 1)
 
-    back = [split_bf16(recv2[a].T) for a in range(2)]
-    back = jnp.concatenate(
-        [back[0][0], back[1][0][0:64], back[0][1], back[1][1][0:64]], axis=0
-    )
+    back_out[...] = recv2[...]
+    out_copy.wait()
+
+
+def finish_kernel(dims, pop_hbm, back_ref, dest_ref, rank_ref, out_hbm, vel_out, held, sems):
+    n_dev, parts = dims
+    f32, bf16, i32 = jnp.float32, jnp.bfloat16, jnp.int32
+    copies_in = [pltpu.make_async_copy(pop_hbm.at[k], held.at[k], sems.at[0, k]) for k in range(19)]
+    copies_out = [
+        pltpu.make_async_copy(held.at[k], out_hbm.at[k], sems.at[1, k]) for k in range(19)
+    ]
+    for copy in copies_in:
+        copy.start()
+    block = min(1024, parts)
+    dev_iota = lax.broadcasted_iota(i32, (n_dev, block), 0)
+    cap_iota = lax.broadcasted_iota(i32, (CAP, block), 0).astype(f32)
+    back = [split_bf16(back_ref[a].T) for a in range(2)]
+    back = jnp.concatenate([back[0][0], back[1][0][0:64], back[0][1], back[1][1][0:64]], axis=0)
 
     def unpack(b, _):
         s = pl.ds(pl.multiple_of(b * block, block), block)
-        found = dot_nn(back, own_hits[:, s])
-        hit = cap_iota == rank_rows[:, s]
+        hits = jnp.where(dev_iota == dest_ref[:, s], 1.0, 0.0).astype(bf16)
+        found = dot_nn(back, hits)
+        hit = cap_iota == rank_ref[:, s]
         for a in range(3):
             value = found[64 * a : 64 * a + 64] + found[64 * (a + 3) : 64 * (a + 3) + 64]
             vel_out[a : a + 1, s] = jnp.sum(jnp.where(hit, value, 0.0), axis=0, keepdims=True)
         return 0
 
-    lax.fori_loop(0, parts // block, unpack, 0)
-    out_copy.wait()
+    blocks = parts // block
+    lax.fori_loop(0, blocks // 4, unpack, 0)
+    for arrived, leaving in zip(copies_in, copies_out):
+        arrived.wait()
+        leaving.start()
+    lax.fori_loop(blocks // 4, blocks, unpack, 0)
+    for copy in copies_out:
+        copy.wait()
 
 
 def per_device(
@@ -589,12 +681,15 @@
     planes = size_x * size_y
     f32, bf16 = jnp.float32, jnp.bfloat16
     vmem = pl.BlockSpec(memory_space=pltpu.VMEM)
-    chunk = min(1024, rows * 128)
-    return pl.pallas_call(
+    chunk = min(2048, rows * 128 // 2)
+    tile = min(1024, rows * 128 // 2)
+    destination = destination.reshape(1, parts)
+    moved, back, ranks = pl.pallas_call(
         functools.partial(kernel, (n_chan, n_width, size_x, size_y, size_z, parts)),
         out_shape=(
             jax.ShapeDtypeStruct(populations.shape, f32),
-            jax.ShapeDtypeStruct(particle_velocity.shape, f32),
+            jax.ShapeDtypeStruct((2, n_dev, 128), f32),
+            jax.ShapeDtypeStruct((1, parts), f32),
         ),
         in_specs=[
             pl.BlockSpec(memory_space=pl.ANY),
@@ -605,28 +700,32 @@
             vmem,
             vmem,
         ],
-        out_specs=(pl.BlockSpec(memory_space=pl.ANY), vmem),
+        out_specs=(pl.BlockSpec(memory_space=pl.ANY), vmem, vmem),
         scratch_shapes=[
-            pltpu.VMEM(populations.shape, f32),
             pltpu.VMEM(populations.shape, f32),
             pltpu.VMEM((2, 16, size_x + 2, size_y + 2 * PAD, size_z), f32),
             pltpu.VMEM((2, 3, size_x, size_y, size_z), f32),
             pltpu.VMEM((n_dev, parts), bf16),
-            pltpu.VMEM((1, parts), f32),
             pltpu.VMEM((10 * CAP, parts), bf16),
             pltpu.VMEM((3, n_dev, 128), f32),
             pltpu.VMEM((3, n_dev, 128), f32),
             pltpu.VMEM((2, n_dev, 128), f32),
             pltpu.VMEM((2, n_dev, 128), f32),
-            pltpu.VMEM((10, rows, 128), f32),
-            pltpu.VMEM((planes, rows * 128), bf16),
+            pltpu.VMEM((4, rows, 128), f32),
+            pltpu.VMEM((2, rows, 128), f32),
+            pltpu.VMEM((4, rows, 128), f32),
+            pltpu.VMEM((3, rows, 128), f32),
+            pltpu.VMEM((2 * planes, rows * 128), bf16),
             pltpu.VMEM((size_z, rows * 128), bf16),
             pltpu.VMEM((8 * size_z, chunk), bf16),
-            pltpu.VMEM((planes, 8 * size_z), f32),
-            pltpu.VMEM((7, planes, size_z), f32),
+            pltpu.VMEM((8 * size_z, chunk), bf16),
+            pltpu.VMEM((8 * size_z, planes), f32),
+            pltpu.VMEM((3 * size_z, tile), f32),
+            pltpu.VMEM((3 * size_z, tile), f32),
+            pltpu.VMEM((10, planes, size_z), f32),
             pltpu.VMEM((STEPS, 3, planes, size_z), f32),
-            pltpu.VMEM((6 * size_z, planes), bf16),
-            pltpu.SMEM((64,), f32),
+            pltpu.VMEM((3 * size_z, 2 * planes), bf16),
+            pltpu.VMEM((51, 8, 128), f32),
             pltpu.SemaphoreType.DMA,
             pltpu.SemaphoreType.DMA,
             pltpu.SemaphoreType.DMA((2,)),
@@ -642,11 +741,26 @@
         populations,
         moment_rates,
         solid_flags,
-        destination.reshape(1, parts),
+        destination,
         local_cell.reshape(1, parts),
         particle_velocity,
         coupling.reshape(1, parts),
     )
+    return pl.pallas_call(
+        functools.partial(finish_kernel, (n_dev, parts)),
+        out_shape=(
+            jax.ShapeDtypeStruct(populations.shape, f32),
+            jax.ShapeDtypeStruct(particle_velocity.shape, f32),
+        ),
+        in_specs=[pl.BlockSpec(memory_space=pl.ANY), vmem, vmem, vmem],
+        out_specs=(pl.BlockSpec(memory_space=pl.ANY), vmem),
+        scratch_shapes=[
+            pltpu.VMEM(populations.shape, f32),
+            pltpu.SemaphoreType.DMA((2, 19)),
+        ],
+        compiler_params=pltpu.CompilerParams(vmem_limit_bytes=56 * 1024 * 1024),
+        name="particles_back",
+    )(moved, back, destination, ranks)
 
 
 def solution(mesh):

time: 115 us -> 98.4 us (0.86)
  Pallas kernels: 110 us -> 97.4 us
  local copies, waits for them, and re-layouts: 4.03 us -> 0 us
    pallas_call x1, Pallas kernels: 110 us -> 92.7 us  [per_device(): pl.pallas_call(functools.partial(kernel, (n_chan, n_width, size_x, size_y...]
    pallas_call x0 -> x1, Pallas kernels: none -> 4.75 us  [per_device(): pl.pallas_call(functools.partial(finish_kernel, (n_dev, parts)), out_shap...]
    unnamed x4 -> x0, local copies, waits for them, and re-layouts: 4.03 us -> none
where the time goes in v1:
time: 98.4 us; the launch traced here: 98.2 us
  Pallas kernels  97.4 us (99%)
    pallas_call x1, Pallas kernels, per_device(): pl.pallas_call(functools.partial(kernel, (n_chan, n_width, size_x, size_y...  92.7 us
    pallas_call x1, Pallas kernels, per_device(): pl.pallas_call(functools.partial(finish_kernel, (n_dev, parts)), out_shap...  4.75 us

profile of v1, /device:TPU:1, one launch (start us, length us, event | category | flops | bytes accessed | tf_op | source)
XLA Modules:
  0.0 98.2 jit_solution(8088754501950434150)
XLA Ops:
  0.6 92.7 %lattice_steps.1 = (f32[19,16,16,128]{3,2,1,0:T(8,128)}, f32[2,128,128]{2,1,0:T(8,128)}, f32[1,4096]{1,0:T(1,128)}) custom-call(f32[19,16,16,128]{3,2,1,0:T(8,128)} %pop_hbm.1, f32[15]{0:T(128)} %rates_ref.1, s32[16,16,128]{2,1,0:T(8,128)} %solid_ref.1, s32[1,4096]{1,0:T(1,128)} %bitcast.3, s32[1,4096]{1,0:T(1,128)} %bitcast.5, f32[3,4096]{1,0:T(4,128)} %vel_ref.1, ...), custom_call_target="tpu_custom_call" | custom-call | tf_op jit(solution)/shard_map/lattice_steps/pallas_call | solution.py:687
  93.3 4.8 %particles_back.1 = (f32[19,16,16,128]{3,2,1,0:T(8,128)}, f32[3,4096]{1,0:T(4,128)}) custom-call(f32[19,16,16,128]{3,2,1,0:T(8,128)} %get-tuple-element.5.pop_hbm, f32[2,128,128]{2,1,0:T(8,128)} %get-tuple-element.6.back_ref, s32[1,4096]{1,0:T(1,128)} %bitcast.4, f32[1,4096]{1,0:T(1,128)} %get-tuple-element.7.rank_ref), custom_call_target="tpu_custom_call" | custom-call | tf_op jit(solution)/shard_map/particles_back/pallas_call | solution.py:749

commit v2 on v1

--- a/solution.py
+++ b/solution.py
@@ -249,6 +249,7 @@
     weights,
     seen,
     plane_hits,
+    slot_hits,
     depth_hits,
     spread_a,
     spread_b,
@@ -276,14 +277,29 @@
 
     barrier = pltpu.get_barrier_semaphore()
 
-    def greet(i, _):
-        o = lax.rem(me + i, n_dev)
-        pl.semaphore_signal(
-            barrier, inc=1, device_id=(o // n_width, lax.rem(o, n_width)), device_id_type=MESH
-        )
-        return 0
-
-    lax.fori_loop(1, n_dev, greet, 0)
+    def wrap(x, n):
+        return jnp.where(x >= n, x - n, x)
+
+    across = [n_width // 2 + (1 - 2 * (j % 2)) * ((j + 1) // 2) for j in range(n_width - 1)] + [0]
+    widths = [wrap(width + d, n_width) for d in across]
+
+    def each_peer(act):
+        def one(j, _):
+            odd = lax.rem(j, 2)
+            d = n_chan // 2 + (1 - 2 * odd) * ((j + odd) // 2)
+            c = wrap(chan + d, n_chan)
+            for w in widths:
+                act(c, w)
+            return 0
+
+        lax.fori_loop(0, n_chan - 1, one, 0, unroll=3)
+        for w in widths[:-1]:
+            act(chan, w)
+
+    def greet(c, w):
+        pl.semaphore_signal(barrier, inc=1, device_id=(c, w), device_id_type=MESH)
+
+    each_peer(greet)
     pop_copy = pltpu.make_async_copy(pop_hbm, pop, pop_sem)
     pop_copy.start()
 
@@ -341,13 +357,14 @@
 
     pl.semaphore_wait(barrier, n_dev - 1)
 
-    def exchange_send(src, dst, which, o):
+    def exchange_send(src, dst, which, c, w):
+        o = c * n_width + w
         pltpu.make_async_remote_copy(
             src.at[:, pl.ds(o, 1)],
             dst.at[:, pl.ds(me, 1)],
             a2a_send.at[which],
             a2a_recv.at[which],
-            device_id=(o // n_width, lax.rem(o, n_width)),
+            device_id=(c, w),
             device_id_type=MESH,
         ).start()
 
@@ -356,11 +373,7 @@
         pltpu.make_async_copy(dst.at[:, part], dst.at[:, part], a2a_recv.at[which]).wait()
         pltpu.make_async_copy(src.at[:, part], src.at[:, part], a2a_send.at[which]).wait()
 
-    def send_one(i, _):
-        exchange_send(send1, recv1, 0, lax.rem(me + i, n_dev))
-        return 0
-
-    lax.fori_loop(1, n_dev, send_one, 0)
+    each_peer(functools.partial(exchange_send, send1, recv1, 0))
     recv1[:, pl.ds(me, 1), :] = send1[:, pl.ds(me, 1), :]
     exchange_wait(send1, recv1, 0)
 
@@ -384,17 +397,24 @@
     weights[3] = coup
 
     plane_iota = lax.broadcasted_iota(i32, (planes, 128), 0).astype(f32)
+    plane_lanes = lax.broadcasted_iota(i32, (128, planes), 1).astype(f32)
     depth_iota = lax.broadcasted_iota(i32, (size_z, 128), 0).astype(f32)
 
-    def place(i, _):
-        s = pl.ds(pl.multiple_of(i * 128, 128), 128)
-        hits = jnp.where(plane_iota == cells[0, pl.ds(i, 1), :], 1.0, 0.0).astype(bf16)
-        plane_hits[0:planes, s] = hits
-        plane_hits[planes : 2 * planes, s] = hits
-        depth_hits[:, s] = jnp.where(depth_iota == cells[1, pl.ds(i, 1), :], 1.0, 0.0).astype(bf16)
+    def place(n, _):
+        columns = cells[0, pl.ds(pl.multiple_of(8 * n, 8), 8), :].T
+        for r in range(8):
+            i = 8 * n + r
+            s = pl.ds(pl.multiple_of(i * 128, 128), 128)
+            hits = jnp.where(plane_iota == cells[0, pl.ds(i, 1), :], 1.0, 0.0).astype(bf16)
+            plane_hits[0:planes, s] = hits
+            plane_hits[planes : 2 * planes, s] = hits
+            hits = jnp.where(depth_iota == cells[1, pl.ds(i, 1), :], 1.0, 0.0)
+            depth_hits[:, s] = hits.astype(bf16)
+            hits = jnp.where(plane_lanes == columns[:, r : r + 1], 1.0, 0.0)
+            slot_hits[s, :] = hits.astype(bf16)
         return 0
 
-    lax.fori_loop(0, rows, place, 0, unroll=2)
+    lax.fori_loop(0, rows // 8, place, 0)
 
     chunk = min(2048, rows * 128 // 2)
     chunk_rows = chunk // 128
@@ -416,24 +436,28 @@
 
     def add_chunk(n, spread):
         s = pl.ds(pl.multiple_of(n * chunk, chunk), chunk)
-        summed[...] += dot_nt(spread[...], plane_hits[0:planes, s])
-
-    def scatter(targets, beside=None):
+        summed[...] += dot_nn(spread[...], slot_hits[s, :])
+
+    def ends_first(i):
+        return jnp.where(i == 0, 0, jnp.where(i == 1, size_x - 1, i - 1))
+
+    def scatter(targets, beside=None, early=None):
         summed[...] = jnp.zeros_like(summed)
-        weigh_chunk(0, spread_a)
         share = size_x // chunks
 
         def two(n, _):
-            weigh_chunk(2 * n + 1, spread_b)
-            add_chunk(2 * n, spread_a)
-            if beside is not None:
-                for i in range(share):
-                    beside(2 * n * share + i)
-            weigh_chunk(lax.rem(2 * n + 2, chunks), spread_a)
-            add_chunk(2 * n + 1, spread_b)
-            if beside is not None:
-                for i in range(share):
-                    beside((2 * n + 1) * share + i)
+            for part, spread in enumerate((spread_a, spread_b)):
+                weigh_chunk(2 * n + part, spread)
+                add_chunk(2 * n + part, spread)
+                if beside is not None:
+                    for i in range(share):
+                        beside(ends_first((2 * n + part) * share + i))
+            if early is not None:
+
+                @pl.when(n == 0)
+                def _():
+                    early()
+
             return 0
 
         lax.fori_loop(0, chunks // 2, two, 0)
@@ -504,11 +528,12 @@
         send2[1, upper, :] = jnp.where(low, pltpu.roll(vz, 64, 1), 0.0)
         for r in range(tile_rows):
             for side in range(2):
-                o = side * half_dev + n * tile_rows + r
-
-                @pl.when(o != me)
+                c = (side * half_dev + r) // n_width + n * (tile_rows // n_width)
+                w = r % n_width
+
+                @pl.when(jnp.logical_or(c != chan, w != width))
                 def _():
-                    exchange_send(send2, recv2, 1, o)
+                    exchange_send(send2, recv2, 1, c, w)
 
     def nb(dc, dw):
         return (lax.rem(chan + dc + n_chan, n_chan), lax.rem(width + dw + n_width, n_width))
@@ -517,7 +542,7 @@
     last_x, last_y = size_x, PAD + size_y - 1
     end_x, end_y = size_x + 1, PAD + size_y
 
-    def halo_copies(t):
+    def halo_copy(t, n):
         g = moved.at[t % 2]
         parts_list = [
             (g.at[0:5, last_x, inner_y], g.at[0:5, 0, inner_y], nb(1, 0)),
@@ -530,12 +555,10 @@
             (g.at[0, last_x, pl.ds(PAD, 1)], g.at[0, 0, pl.ds(end_y, 1)], nb(1, -1)),
             (g.at[8, 1, pl.ds(last_y, 1)], g.at[8, end_x, pl.ds(PAD - 1, 1)], nb(-1, 1)),
         ]
-        return [
-            pltpu.make_async_remote_copy(
-                src, dst, halo_send.at[t, n], halo_recv.at[t, n], device_id=to, device_id_type=MESH
-            )
-            for n, (src, dst, to) in enumerate(parts_list)
-        ]
+        src, dst, to = parts_list[n]
+        return pltpu.make_async_remote_copy(
+            src, dst, halo_send.at[t, n], halo_recv.at[t, n], device_id=to, device_id_type=MESH
+        )
 
     def load(t, i, h):
         f = []
@@ -587,29 +610,36 @@
     pop_copy.wait()
     for t in range(STEPS):
         plane = step_plane(t)
+
+        def send_ends():
+            for n in (5, 6, 7, 8, 0, 1):
+                halo_copy(t, n).start()
+
         if t < STEPS - 1:
             for a in range(3):
                 weights[a] = weights[a] * keep
             if t > 0:
                 weights[3] = weights[3] * keep
             odd = (t + 1) % 2
-            scatter([1 + 3 * odd, 2 + 3 * odd, 3 + 3 * odd, 7 + t], plane)
+            scatter([1 + 3 * odd, 2 + 3 * odd, 3 + 3 * odd, 7 + t], plane, send_ends)
         else:
 
             def one(i, _):
                 plane(i)
                 return 0
 
-            lax.fori_loop(0, size_x, one, 0)
-        copies = halo_copies(t)
-        for copy in copies:
-            copy.start()
+            plane(0)
+            plane(size_x - 1)
+            send_ends()
+            lax.fori_loop(1, size_x - 1, one, 0, unroll=2)
+        for n in (2, 3, 4):
+            halo_copy(t, n).start()
         if t < STEPS - 1:
             gather(t)
         else:
             gather(t, deliver)
-        for copy in copies:
-            copy.wait()
+        for n in range(9):
+            halo_copy(t, n).wait()
 
     def finish(i, _):
         for h in range(size_y // 8):
@@ -716,6 +746,7 @@
             pltpu.VMEM((4, rows, 128), f32),
             pltpu.VMEM((3, rows, 128), f32),
             pltpu.VMEM((2 * planes, rows * 128), bf16),
+            pltpu.VMEM((rows * 128, planes), bf16),
             pltpu.VMEM((size_z, rows * 128), bf16),
             pltpu.VMEM((8 * size_z, chunk), bf16),
             pltpu.VMEM((8 * size_z, chunk), bf16),

time: 98.4 us -> 89 us (0.904)
  Pallas kernels: 97.4 us -> 88 us
    pallas_call x1, Pallas kernels: 92.7 us -> 83.3 us  [per_device(): pl.pallas_call(functools.partial(kernel, (n_chan, n_width, size_x, size_y...]
where the time goes in v2:
time: 89 us; the launch traced here: 88.8 us
  Pallas kernels  88 us (99%)
    pallas_call x1, Pallas kernels, per_device(): pl.pallas_call(functools.partial(kernel, (n_chan, n_width, size_x, size_y...  83.3 us
    pallas_call x1, Pallas kernels, per_device(): pl.pallas_call(functools.partial(finish_kernel, (n_dev, parts)), out_shap...  4.75 us

profile of v2, /device:TPU:1, one launch (start us, length us, event | category | flops | bytes accessed | tf_op | source)
XLA Modules:
  0.0 88.8 jit_solution(7584319613356121967)
XLA Ops:
  0.6 83.3 %lattice_steps.1 = (f32[19,16,16,128]{3,2,1,0:T(8,128)}, f32[2,128,128]{2,1,0:T(8,128)}, f32[1,4096]{1,0:T(1,128)}) custom-call(f32[19,16,16,128]{3,2,1,0:T(8,128)} %pop_hbm.1, f32[15]{0:T(128)} %rates_ref.1, s32[16,16,128]{2,1,0:T(8,128)} %solid_ref.1, s32[1,4096]{1,0:T(1,128)} %bitcast.3, s32[1,4096]{1,0:T(1,128)} %bitcast.5, f32[3,4096]{1,0:T(4,128)} %vel_ref.1, ...), custom_call_target="tpu_custom_call" | custom-call | tf_op jit(solution)/shard_map/lattice_steps/pallas_call | solution.py:717
  83.9 4.7 %particles_back.1 = (f32[19,16,16,128]{3,2,1,0:T(8,128)}, f32[3,4096]{1,0:T(4,128)}) custom-call(f32[19,16,16,128]{3,2,1,0:T(8,128)} %get-tuple-element.5.pop_hbm, f32[2,128,128]{2,1,0:T(8,128)} %get-tuple-element.6.back_ref, s32[1,4096]{1,0:T(1,128)} %bitcast.4, f32[1,4096]{1,0:T(1,128)} %get-tuple-element.7.rank_ref), custom_call_target="tpu_custom_call" | custom-call | tf_op jit(solution)/shard_map/particles_back/pallas_call | solution.py:780

commit v3 on v2

--- a/solution.py
+++ b/solution.py
@@ -12,6 +12,7 @@
 MESH = pl.DeviceIdType.MESH
 STEPS = 4
 CAP = 64
+PIECES = 4
 LATTICE = [
     [0, 0, 0],
     [1, 0, 0],
@@ -251,8 +252,7 @@
     plane_hits,
     slot_hits,
     depth_hits,
-    spread_a,
-    spread_b,
+    spread,
     summed,
     found_a,
     found_b,
@@ -336,15 +336,16 @@
         rank_rows[:, s] = rank
         rank_hit = cap_iota == rank
         cell = cell_ref[:, s]
-        pieces = []
+        mask = jnp.where(rank_hit, 1.0, 0.0).astype(bf16).reshape(CAP // 16, 16, block)
+        pairs = []
         for value in (coup_ref[:, s], vel_ref[0:1, s], vel_ref[1:2, s], vel_ref[2:3, s]):
-            pieces.append(split_bf16(value))
-        order = [pieces[0][0], pieces[1][0], pieces[0][1], pieces[1][1]]
-        order += [pieces[2][0], pieces[3][0], pieces[2][1], pieces[3][1]]
-        order = [piece.astype(f32) for piece in order]
-        order += [(cell // 128).astype(f32), lax.rem(cell, 128).astype(f32)]
+            pairs.append(split_bf16(jnp.broadcast_to(value, (16, block))))
+        order = [pairs[0][0], pairs[1][0], pairs[0][1], pairs[1][1]]
+        order += [pairs[2][0], pairs[3][0], pairs[2][1], pairs[3][1]]
+        for part in (cell // 128, lax.rem(cell, 128)):
+            order.append(jnp.broadcast_to(part.astype(f32), (16, block)).astype(bf16))
         for j, row in enumerate(order):
-            packing[j * CAP : (j + 1) * CAP, s] = jnp.where(rank_hit, row, 0.0).astype(bf16)
+            packing[j * CAP : (j + 1) * CAP, s] = (mask * row[None]).reshape(CAP, block)
         return before + upto[:, block - 1 : block]
 
     lax.fori_loop(0, parts // block, pack, jnp.zeros((n_dev, 1), f32), unroll=4)
@@ -396,30 +397,36 @@
     weights[0], weights[1], weights[2] = coup * vx, coup * vy, coup * vz
     weights[3] = coup
 
-    plane_iota = lax.broadcasted_iota(i32, (planes, 128), 0).astype(f32)
-    plane_lanes = lax.broadcasted_iota(i32, (128, planes), 1).astype(f32)
+    plane_iota = lax.broadcasted_iota(i32, (planes, 128), 0).astype(f32).astype(bf16)
+    plane_iota = plane_iota.reshape(planes // 16, 16, 128)
+    plane_lanes = lax.broadcasted_iota(i32, (128, planes), 1).astype(f32).astype(bf16)
+    depth_iota_b = lax.broadcasted_iota(i32, (size_z, 128), 0).astype(f32).astype(bf16)
+    depth_iota_b = depth_iota_b.reshape(size_z // 16, 16, 128)
     depth_iota = lax.broadcasted_iota(i32, (size_z, 128), 0).astype(f32)
 
-    def place(n, _):
+    one, zero = jnp.bfloat16(1.0), jnp.bfloat16(0.0)
+
+    def row_of(which, i):
+        return jnp.broadcast_to(cells[which, pl.ds(i, 1), :], (16, 128)).astype(bf16)[None]
+
+    def place(n):
         columns = cells[0, pl.ds(pl.multiple_of(8 * n, 8), 8), :].T
         for r in range(8):
             i = 8 * n + r
             s = pl.ds(pl.multiple_of(i * 128, 128), 128)
-            hits = jnp.where(plane_iota == cells[0, pl.ds(i, 1), :], 1.0, 0.0).astype(bf16)
+            hits = jnp.where(plane_iota == row_of(0, i), one, zero).reshape(planes, 128)
             plane_hits[0:planes, s] = hits
             plane_hits[planes : 2 * planes, s] = hits
-            hits = jnp.where(depth_iota == cells[1, pl.ds(i, 1), :], 1.0, 0.0)
-            depth_hits[:, s] = hits.astype(bf16)
-            hits = jnp.where(plane_lanes == columns[:, r : r + 1], 1.0, 0.0)
-            slot_hits[s, :] = hits.astype(bf16)
-        return 0
-
-    lax.fori_loop(0, rows // 8, place, 0)
-
-    chunk = min(2048, rows * 128 // 2)
+            hits = jnp.where(depth_iota_b == row_of(1, i), one, zero).reshape(size_z, 128)
+            depth_hits[:, s] = hits
+            column = jnp.broadcast_to(columns[:, r : r + 1], (128, planes)).astype(bf16)
+            slot_hits[s, :] = jnp.where(plane_lanes == column, one, zero)
+
+    chunk = 1024
     chunk_rows = chunk // 128
 
     chunks = rows // chunk_rows
+    pieces = min(PIECES, chunks)
 
     def weigh_chunk(n, spread):
         for r in range(chunk_rows):
@@ -441,17 +448,20 @@
     def ends_first(i):
         return jnp.where(i == 0, 0, jnp.where(i == 1, size_x - 1, i - 1))
 
-    def scatter(targets, beside=None, early=None):
+    def scatter(targets, before=None, beside=None, early=None):
         summed[...] = jnp.zeros_like(summed)
         share = size_x // chunks
 
-        def two(n, _):
-            for part, spread in enumerate((spread_a, spread_b)):
-                weigh_chunk(2 * n + part, spread)
-                add_chunk(2 * n + part, spread)
+        def some(n, _):
+            for part in range(pieces):
+                p = pieces * n + part
+                if before is not None:
+                    before(p)
+                weigh_chunk(p, spread.at[part])
+                add_chunk(p, spread.at[part])
                 if beside is not None:
                     for i in range(share):
-                        beside(ends_first((2 * n + part) * share + i))
+                        beside(ends_first(p * share + i))
             if early is not None:
 
                 @pl.when(n == 0)
@@ -460,7 +470,7 @@
 
             return 0
 
-        lax.fori_loop(0, chunks // 2, two, 0)
+        lax.fori_loop(0, chunks // pieces, some, 0)
         for j, target in enumerate(targets):
             at = 2 * j * size_z
             total = summed[at : at + size_z, :] + summed[at + size_z : at + 2 * size_z, :]
@@ -495,26 +505,29 @@
         def turn(n):
             return n if then is None else lax.rem(n + first_tile, tiles)
 
+        def use(n, found, own=False):
+            pick(turn(n), found)
+            if then is not None:
+                then(turn(n), own)
+
         find(turn(0), found_a)
+        find(turn(1), found_b)
+        use(0, found_a, True)
 
         def two(n, _):
-            first, second, third = turn(2 * n), turn(2 * n + 1), turn(lax.rem(2 * n + 2, tiles))
-            find(second, found_b)
-            pick(first, found_a)
-            if then is not None:
-                then(first)
-            find(third, found_a)
-            pick(second, found_b)
-            if then is not None:
-                then(second)
+            find(turn(2 * n + 2), found_a)
+            use(2 * n + 1, found_b)
+            find(turn(2 * n + 3), found_b)
+            use(2 * n + 2, found_a)
             return 0
 
-        lax.fori_loop(0, tiles // 2, two, 0)
+        lax.fori_loop(0, tiles // 2 - 1, two, 0)
+        use(tiles - 1, found_b)
         if then is None:
             for a in range(3):
                 slots[1 + a] = slots[1 + a] + slots[0] * (seen[a] - slots[1 + a])
 
-    def deliver(n):
+    def deliver(n, own):
         s = pl.ds(pl.multiple_of(n * tile_rows, tile_rows), tile_rows)
         upper = pl.ds(pl.multiple_of(half_dev + n * tile_rows, tile_rows), tile_rows)
         low = lax.broadcasted_iota(i32, (tile_rows, 128), 1) < 64
@@ -531,8 +544,13 @@
                 c = (side * half_dev + r) // n_width + n * (tile_rows // n_width)
                 w = r % n_width
 
-                @pl.when(jnp.logical_or(c != chan, w != width))
-                def _():
+                if own:
+
+                    @pl.when(jnp.logical_or(c != chan, w != width))
+                    def _():
+                        exchange_send(send2, recv2, 1, c, w)
+
+                else:
                     exchange_send(send2, recv2, 1, c, w)
 
     def nb(dc, dw):
@@ -603,7 +621,7 @@
 
         return one
 
-    scatter([1, 2, 3, 0])
+    scatter([1, 2, 3, 0], before=place)
     coup = slots[0]
     keep = 1.0 - coup
     weights[3] = coup * coup
@@ -621,7 +639,7 @@
             if t > 0:
                 weights[3] = weights[3] * keep
             odd = (t + 1) % 2
-            scatter([1 + 3 * odd, 2 + 3 * odd, 3 + 3 * odd, 7 + t], plane, send_ends)
+            scatter([1 + 3 * odd, 2 + 3 * odd, 3 + 3 * odd, 7 + t], None, plane, send_ends)
         else:
 
             def one(i, _):
@@ -711,7 +729,7 @@
     planes = size_x * size_y
     f32, bf16 = jnp.float32, jnp.bfloat16
     vmem = pl.BlockSpec(memory_space=pltpu.VMEM)
-    chunk = min(2048, rows * 128 // 2)
+    chunk = 1024
     tile = min(1024, rows * 128 // 2)
     destination = destination.reshape(1, parts)
     moved, back, ranks = pl.pallas_call(
@@ -748,8 +766,7 @@
             pltpu.VMEM((2 * planes, rows * 128), bf16),
             pltpu.VMEM((rows * 128, planes), bf16),
             pltpu.VMEM((size_z, rows * 128), bf16),
-            pltpu.VMEM((8 * size_z, chunk), bf16),
-            pltpu.VMEM((8 * size_z, chunk), bf16),
+            pltpu.VMEM((PIECES, 8 * size_z, chunk), bf16),
             pltpu.VMEM((8 * size_z, planes), f32),
             pltpu.VMEM((3 * size_z, tile), f32),
             pltpu.VMEM((3 * size_z, tile), f32),

time: 89 us -> 83.7 us (0.940)
  Pallas kernels: 88 us -> 82.7 us
    pallas_call x1, Pallas kernels: 83.3 us -> 78 us  [per_device(): pl.pallas_call(functools.partial(kernel, (n_chan, n_width, size_x, size_y...]
where the time goes in v3:
time: 83.7 us; the launch traced here: 83.5 us
  Pallas kernels  82.7 us (99%)
    pallas_call x1, Pallas kernels, per_device(): pl.pallas_call(functools.partial(kernel, (n_chan, n_width, size_x, size_y...  78 us
    pallas_call x1, Pallas kernels, per_device(): pl.pallas_call(functools.partial(finish_kernel, (n_dev, parts)), out_shap...  4.75 us

profile of v3, /device:TPU:1, one launch (start us, length us, event | category | flops | bytes accessed | tf_op | source)
XLA Modules:
  0.0 83.5 jit_solution(2466205683313871337)
XLA Ops:
  0.6 78.0 %lattice_steps.1 = (f32[19,16,16,128]{3,2,1,0:T(8,128)}, f32[2,128,128]{2,1,0:T(8,128)}, f32[1,4096]{1,0:T(1,128)}) custom-call(f32[19,16,16,128]{3,2,1,0:T(8,128)} %pop_hbm.1, f32[15]{0:T(128)} %rates_ref.1, s32[16,16,128]{2,1,0:T(8,128)} %solid_ref.1, s32[1,4096]{1,0:T(1,128)} %bitcast.3, s32[1,4096]{1,0:T(1,128)} %bitcast.5, f32[3,4096]{1,0:T(4,128)} %vel_ref.1, ...), custom_call_target="tpu_custom_call" | custom-call | tf_op jit(solution)/shard_map/lattice_steps/pallas_call | solution.py:735
  78.6 4.7 %particles_back.1 = (f32[19,16,16,128]{3,2,1,0:T(8,128)}, f32[3,4096]{1,0:T(4,128)}) custom-call(f32[19,16,16,128]{3,2,1,0:T(8,128)} %get-tuple-element.5.pop_hbm, f32[2,128,128]{2,1,0:T(8,128)} %get-tuple-element.6.back_ref, s32[1,4096]{1,0:T(1,128)} %bitcast.4, f32[1,4096]{1,0:T(1,128)} %get-tuple-element.7.rank_ref), custom_call_target="tpu_custom_call" | custom-call | tf_op jit(solution)/shard_map/particles_back/pallas_call | solution.py:797

commit v4 on v3

--- a/solution.py
+++ b/solution.py
@@ -228,17 +228,24 @@
     dims,
     pop_hbm,
     rates_ref,
+    solid_hbm,
+    dest_hbm,
+    cell_hbm,
+    vel_hbm,
+    coup_hbm,
+    out_hbm,
+    back_out,
+    rank_rows,
+    pop,
     solid_ref,
     dest_ref,
     cell_ref,
     vel_ref,
     coup_ref,
-    out_hbm,
-    back_out,
-    rank_rows,
-    pop,
-    moved,
-    stayed,
+    moved_even,
+    moved_odd,
+    stayed_even,
+    stayed_odd,
     own_hits,
     packing,
     send1,
@@ -257,10 +264,14 @@
     found_a,
     found_b,
     fields,
-    mom,
+    mom_0,
+    mom_1,
+    mom_2,
+    mom_3,
     mom_t,
     coef_ref,
     pop_sem,
+    in_sems,
     out_sem,
     a2a_send,
     a2a_recv,
@@ -275,6 +286,16 @@
     me = chan * n_width + width
     f32, bf16, i32 = jnp.float32, jnp.bfloat16, jnp.int32
 
+    moved, stayed = (moved_even, moved_odd), (stayed_even, stayed_odd)
+    mom = (mom_0, mom_1, mom_2, mom_3)
+    small = [(dest_hbm, dest_ref), (cell_hbm, cell_ref), (vel_hbm, vel_ref), (coup_hbm, coup_ref)]
+    small.append((solid_hbm, solid_ref))
+    small = [pltpu.make_async_copy(a, b, in_sems.at[n]) for n, (a, b) in enumerate(small)]
+    for copy in small:
+        copy.start()
+    pop_copy = pltpu.make_async_copy(pop_hbm, pop, pop_sem)
+    pop_copy.start()
+
     barrier = pltpu.get_barrier_semaphore()
 
     def wrap(x, n):
@@ -300,8 +321,6 @@
         pl.semaphore_signal(barrier, inc=1, device_id=(c, w), device_id_type=MESH)
 
     each_peer(greet)
-    pop_copy = pltpu.make_async_copy(pop_hbm, pop, pop_sem)
-    pop_copy.start()
 
     even_table, odd_tables, cross_table = sector_tables()
     rates = [jnp.full((8, 128), rates_ref[j], f32) for j in range(15)]
@@ -319,6 +338,8 @@
         coef_ref[places] = weigh(rates, cross_table[g])
         places += 1
 
+    for copy in small[:4]:
+        copy.wait()
     block = 256
     tri = (
         lax.broadcasted_iota(i32, (block, block), 0) <= lax.broadcasted_iota(i32, (block, block), 1)
@@ -448,7 +469,7 @@
     def ends_first(i):
         return jnp.where(i == 0, 0, jnp.where(i == 1, size_x - 1, i - 1))
 
-    def scatter(targets, before=None, beside=None, early=None):
+    def scatter(targets, before=None, beside=None, early=None, late=None):
         summed[...] = jnp.zeros_like(summed)
         share = size_x // chunks
 
@@ -471,6 +492,8 @@
             return 0
 
         lax.fori_loop(0, chunks // pieces, some, 0)
+        if late is not None:
+            late()
         for j, target in enumerate(targets):
             at = 2 * j * size_z
             total = summed[at : at + size_z, :] + summed[at + size_z : at + 2 * size_z, :]
@@ -498,7 +521,7 @@
 
     def gather(t, then=None):
         for a in range(3):
-            hi, lo = split_bf16(mom[t, a].T)
+            hi, lo = split_bf16(mom[t][a].T)
             mom_t[a * size_z : (a + 1) * size_z, 0:planes] = hi
             mom_t[a * size_z : (a + 1) * size_z, planes : 2 * planes] = lo
 
@@ -561,7 +584,7 @@
     end_x, end_y = size_x + 1, PAD + size_y
 
     def halo_copy(t, n):
-        g = moved.at[t % 2]
+        g = moved[t % 2]
         parts_list = [
             (g.at[0:5, last_x, inner_y], g.at[0:5, 0, inner_y], nb(1, 0)),
             (g.at[8:13, 1, inner_y], g.at[8:13, end_x, inner_y], nb(-1, 0)),
@@ -584,11 +607,11 @@
             if t == 0:
                 f.append(pop[k, i, 8 * h : 8 * h + 8, :])
             elif k in STAY:
-                f.append(stayed[(t - 1) % 2, STAY[k], i, 8 * h : 8 * h + 8, :])
+                f.append(stayed[(t - 1) % 2][STAY[k], i, 8 * h : 8 * h + 8, :])
             else:
                 step_x, step_y, _ = LATTICE[k]
                 start = PAD + 8 * h - step_y
-                f.append(moved[(t - 1) % 2, SLOT_OF[k], i + 1 - step_x, start : start + 8, :])
+                f.append(moved[(t - 1) % 2][SLOT_OF[k], i + 1 - step_x, start : start + 8, :])
         return f
 
     def step_plane(t):
@@ -605,19 +628,19 @@
                 count = fields[0, at, :]
                 held = [fields[1 + 3 * (t % 2) + a, at, :] for a in range(3)]
                 memory = [fields[7 + t - 1 - s, at, :] for s in range(t)]
-                seen_m = [[mom[s, a, at, :] for a in range(3)] for s in range(t)]
+                seen_m = [[mom[s][a, at, :] for a in range(3)] for s in range(t)]
                 solid = solid_ref[i, 8 * h : 8 * h + 8, :] == 1
                 out, m = relax_group(f, (count, held, memory), seen_m, solid, coefs)
                 for a in range(3):
-                    mom[t, a, at, :] = m[a]
+                    mom[t][a, at, :] = m[a]
                 for k in range(19):
                     value = out[k]
                     if LATTICE[k][2]:
                         value = pltpu.roll(value, LATTICE[k][2] % size_z, 1)
                     if k in STAY:
-                        stayed[t % 2, STAY[k], i, 8 * h : 8 * h + 8, :] = value
+                        stayed[t % 2][STAY[k], i, 8 * h : 8 * h + 8, :] = value
                     else:
-                        moved[t % 2, SLOT_OF[k], i + 1, PAD + 8 * h : PAD + 8 * h + 8, :] = value
+                        moved[t % 2][SLOT_OF[k], i + 1, PAD + 8 * h : PAD + 8 * h + 8, :] = value
 
         return one
 
@@ -626,11 +649,16 @@
     keep = 1.0 - coup
     weights[3] = coup * coup
     pop_copy.wait()
+    small[4].wait()
     for t in range(STEPS):
         plane = step_plane(t)
 
         def send_ends():
             for n in (5, 6, 7, 8, 0, 1):
+                halo_copy(t, n).start()
+
+        def send_sides():
+            for n in (2, 3, 4):
                 halo_copy(t, n).start()
 
         if t < STEPS - 1:
@@ -639,7 +667,7 @@
             if t > 0:
                 weights[3] = weights[3] * keep
             odd = (t + 1) % 2
-            scatter([1 + 3 * odd, 2 + 3 * odd, 3 + 3 * odd, 7 + t], None, plane, send_ends)
+            scatter([1 + 3 * odd, 2 + 3 * odd, 3 + 3 * odd, 7 + t], None, plane, send_ends, send_sides)
         else:
 
             def one(i, _):
@@ -650,8 +678,7 @@
             plane(size_x - 1)
             send_ends()
             lax.fori_loop(1, size_x - 1, one, 0, unroll=2)
-        for n in (2, 3, 4):
-            halo_copy(t, n).start()
+            send_sides()
         if t < STEPS - 1:
             gather(t)
         else:
@@ -742,17 +769,20 @@
         in_specs=[
             pl.BlockSpec(memory_space=pl.ANY),
             pl.BlockSpec(memory_space=pltpu.SMEM),
-            vmem,
-            vmem,
-            vmem,
-            vmem,
-            vmem,
-        ],
+        ]
+        + [pl.BlockSpec(memory_space=pl.ANY)] * 5,
         out_specs=(pl.BlockSpec(memory_space=pl.ANY), vmem, vmem),
         scratch_shapes=[
             pltpu.VMEM(populations.shape, f32),
-            pltpu.VMEM((2, 16, size_x + 2, size_y + 2 * PAD, size_z), f32),
-            pltpu.VMEM((2, 3, size_x, size_y, size_z), f32),
+            pltpu.VMEM(solid_flags.shape, jnp.int32),
+            pltpu.VMEM((1, parts), jnp.int32),
+            pltpu.VMEM((1, parts), jnp.int32),
+            pltpu.VMEM(particle_velocity.shape, f32),
+            pltpu.VMEM((1, parts), f32),
+            pltpu.VMEM((16, size_x + 2, size_y + 2 * PAD, size_z), f32),
+            pltpu.VMEM((16, size_x + 2, size_y + 2 * PAD, size_z), f32),
+            pltpu.VMEM((3, size_x, size_y, size_z), f32),
+            pltpu.VMEM((3, size_x, size_y, size_z), f32),
             pltpu.VMEM((n_dev, parts), bf16),
             pltpu.VMEM((10 * CAP, parts), bf16),
             pltpu.VMEM((3, n_dev, 128), f32),
@@ -771,10 +801,14 @@
             pltpu.VMEM((3 * size_z, tile), f32),
             pltpu.VMEM((3 * size_z, tile), f32),
             pltpu.VMEM((10, planes, size_z), f32),
-            pltpu.VMEM((STEPS, 3, planes, size_z), f32),
+            pltpu.VMEM((3, planes, size_z), f32),
+            pltpu.VMEM((3, planes, size_z), f32),
+            pltpu.VMEM((3, planes, size_z), f32),
+            pltpu.VMEM((3, planes, size_z), f32),
             pltpu.VMEM((3 * size_z, 2 * planes), bf16),
             pltpu.VMEM((51, 8, 128), f32),
             pltpu.SemaphoreType.DMA,
+            pltpu.SemaphoreType.DMA((5,)),
             pltpu.SemaphoreType.DMA,
             pltpu.SemaphoreType.DMA((2,)),
             pltpu.SemaphoreType.DMA((2,)),

time: 83.7 us -> 82.7 us (0.988)
  Pallas kernels: 82.7 us -> 81.7 us
    pallas_call x1, Pallas kernels: 78 us -> 77 us  [per_device(): pl.pallas_call(functools.partial(kernel, (n_chan, n_width, size_x, size_y...]
where the time goes in v4:
time: 82.7 us; the launch traced here: 82.5 us
  Pallas kernels  81.7 us (99%)
    pallas_call x1, Pallas kernels, per_device(): pl.pallas_call(functools.partial(kernel, (n_chan, n_width, size_x, size_y...  77 us
    pallas_call x1, Pallas kernels, per_device(): pl.pallas_call(functools.partial(finish_kernel, (n_dev, parts)), out_shap...  4.75 us

profile of v4, /device:TPU:1, one launch (start us, length us, event | category | flops | bytes accessed | tf_op | source)
XLA Modules:
  0.0 82.5 jit_solution(17480438650987584683)
XLA Ops:
  0.6 77.0 %lattice_steps.1 = (f32[19,16,16,128]{3,2,1,0:T(8,128)}, f32[2,128,128]{2,1,0:T(8,128)}, f32[1,4096]{1,0:T(1,128)}) custom-call(f32[19,16,16,128]{3,2,1,0:T(8,128)} %pop_hbm.1, f32[15]{0:T(128)} %rates_ref.1, s32[16,16,128]{2,1,0:T(8,128)} %solid_hbm.1, s32[1,4096]{1,0:T(1,128)} %bitcast.3, s32[1,4096]{1,0:T(1,128)} %bitcast.5, f32[3,4096]{1,0:T(4,128)} %vel_hbm.1, ...), custom_call_target="tpu_custom_call" | custom-call | tf_op jit(solution)/shard_map/lattice_steps/pallas_call | solution.py:762
  77.6 4.7 %particles_back.1 = (f32[19,16,16,128]{3,2,1,0:T(8,128)}, f32[3,4096]{1,0:T(4,128)}) custom-call(f32[19,16,16,128]{3,2,1,0:T(8,128)} %get-tuple-element.5.pop_hbm, f32[2,128,128]{2,1,0:T(8,128)} %get-tuple-element.6.back_ref, s32[1,4096]{1,0:T(1,128)} %bitcast.4, f32[1,4096]{1,0:T(1,128)} %get-tuple-element.7.rank_ref), custom_call_target="tpu_custom_call" | custom-call | tf_op jit(solution)/shard_map/particles_back/pallas_call | solution.py:831
